TPU v7x, 32 devices: a whole 2x2x4 slice. The times are simulated.
32 devices in a mesh: groups: 2 (over x), expert: 8 (over z, y), tensor: 2 (over core).
Axes of the slice: x: 2, y: 2, z: 4, core: 2. Of those that a mesh axis runs over, the one named last changes fastest.
Arguments:
- tokens: bfloat16 [8192, 2048], P(('groups', 'expert', 'tensor')), parts along dimension 0, may hold values from -6 to 6
- routes: int32 [8192, 4], P(('groups', 'expert', 'tensor')), parts along dimension 0, may hold values from 0 to 7, all different within a row; in each aligned block of 256 rows (0 to 255, 256 to 511, ...) at most 128 rows name the same one
- gates: int32 [8192, 4], P(('groups', 'expert', 'tensor')), parts along dimension 0, may hold values from 1 to 4095
- w_gate: bfloat16 [8, 2048, 1408], P('expert', None, 'tensor'), may hold values from -0.125 to 0.125
- w_up: bfloat16 [8, 2048, 1408], P('expert', None, 'tensor'), may hold values from -0.125 to 0.125
- w_down: bfloat16 [8, 1408, 2048], P('expert', 'tensor'), may hold values from -0.15625 to 0.15625
Outputs:
- mixed: bfloat16 [8192, 2048], P(('groups', 'expert', 'tensor')), parts along dimension 0
There are 2 independent parts, one for each index of `groups`. A program takes and returns all parts, laid end to end along the dimension named above; an argument that names none is the same for every part. Nothing has to cross between parts.
Inputs may be any that keep to these rules, and one draw needn't show every extreme that they name: `routes`: each row names 4 different experts. Of one device's 256 rows at most 128 name any one expert, a bound that some block reaches of them.
All inputs are finite; a program needn't handle non-finite values.
Results may differ from a plain program's by a relative error of at most 0.0066.
Values may be sent and summed in bfloat16 or wider, within the bound.
A program may use at most 128 MiB of HBM per device.

v0:
```python
import jax
import jax.numpy as jnp
from jax import lax
from jax.sharding import PartitionSpec as P

TOPK = 4


def swiglu(row_block, gate_proj, up_proj):
    gate_act = jnp.dot(row_block, gate_proj, preferred_element_type=jnp.float32)
    up_act = jnp.dot(row_block, up_proj, preferred_element_type=jnp.float32)
    return (jax.nn.silu(gate_act) * up_act).astype(jnp.bfloat16)


def rounded_term(hidden, down_proj):
    return jnp.dot(hidden, down_proj, preferred_element_type=jnp.float32).astype(jnp.bfloat16)


def on_device(tokens, routes, gates, w_gate, w_up, w_down):
    tok_dev, features = tokens.shape
    experts = lax.axis_size("expert")
    capacity = max(5 * tok_dev // 16, TOPK * tok_dev // experts)
    gate_proj = w_gate[0]
    up_proj = w_up[0]
    down_proj = w_down[0]
    pair_expert = routes.reshape(-1)
    onehot = (pair_expert[:, None] == jnp.arange(experts, dtype=jnp.int32)[None, :]).astype(
        jnp.int32
    )
    rank_in = jnp.sum((jnp.cumsum(onehot, axis=0) - onehot) * onehot, axis=1)
    slot_index = (pair_expert * capacity + rank_in).reshape(tok_dev, TOPK)
    all_slots = jnp.arange(experts * capacity, dtype=jnp.int32)
    selector = jnp.any(slot_index[None, :, :] == all_slots[:, None, None], axis=2).astype(
        jnp.bfloat16
    )
    outgoing = jnp.dot(selector, tokens, preferred_element_type=jnp.float32).astype(jnp.bfloat16)
    outgoing = outgoing.reshape(experts, capacity, features)
    arrived = lax.all_to_all(outgoing, "expert", split_axis=0, concat_axis=0, tiled=True)
    hidden = swiglu(
        lax.all_gather(arrived.reshape(experts * capacity, features), "tensor", axis=0, tiled=True),
        gate_proj,
        up_proj,
    )
    term = lax.optimization_barrier(rounded_term(hidden, down_proj))
    summed = lax.psum_scatter(
        term.astype(jnp.float32).astype(jnp.bfloat16), "tensor", scatter_dimension=0, tiled=True
    )
    outputs = summed.reshape(experts, capacity, features)
    returned = lax.all_to_all(outputs, "expert", split_axis=0, concat_axis=0, tiled=True)
    weights = gates.astype(jnp.float32)
    weights = weights / jnp.sum(weights, axis=1, keepdims=True)
    flat_back = returned.reshape(experts * capacity, features)
    picked = jnp.take(flat_back, slot_index.reshape(-1), axis=0).reshape(tok_dev, TOPK, features)
    mixed = jnp.sum(picked.astype(jnp.float32) * weights[:, :, None], axis=1)
    return mixed.astype(jnp.bfloat16)


def solution(mesh):
    in_specs = (
        P(("groups", "expert", "tensor"), None),
        P(("groups", "expert", "tensor"), None),
        P(("groups", "expert", "tensor"), None),
        P("expert", None, "tensor"),
        P("expert", None, "tensor"),
        P("expert", "tensor", None),
    )
    out_specs = P(("groups", "expert", "tensor"), None)
    return jax.shard_map(
        on_device, mesh=mesh, in_specs=in_specs, out_specs=out_specs, check_vma=False
    )
```

profile of v0, /device:TPU:0, one launch (start us, length us, event | category | flops | bytes accessed | tf_op | source)
XLA Modules:
  0.0 319.0 jit_solution(681888626583253232)
XLA Ops:
  6.5 1.0 copy.19
  7.5 0.1 eq.39
  7.8 2.3 reduce-window.6
  10.0 0.3 slice_reduce_fusion
  10.3 0.2 reduce-window.9
  10.6 0.1 reduce_sum.32
  10.8 0.7 compare_and_fusion
  11.5 1.0 fusion
  12.5 2.5 convolution_convert_fusion.1
  15.0 100.4 %all_to_all.10 = bf16[8,128,2048]{2,1,0:T(8,128)(2,1)} all-to-all(bf16[8,128,2048]{2,1,0:T(8,128)(2,1)S(1)} %bitcast.39), channel_id=1, replica_groups=mesh['groups'=2,'expert'=8,'tensor'=2] {'expert'}, dimensions={0} | all-to-all | bytes 8388608 | tf_op jit(solution)/shard_map/all_to_all | solution.py:38
  115.4 0.2 reduce-scatter.2.cloned.1.call-start
  115.6 18.8 %all-gather.2.cloned.1.call-done = bf16[2048,2048]{1,0:T(8,128)(2,1)} async-done(((bf16[1024,2048]{1,0:T(8,128)(2,1)}), bf16[2048,2048]{1,0:T(8,128)(2,1)}) %all-gather.2.cloned.1.call-update) | async-done | bytes 8388624 | tf_op jit(solution)/shard_map/all_gather | solution.py:40
  134.4 11.0 %fusion.4 = f32[2048,704]{0,1:T(8,128)} fusion(bf16[2048,2048]{1,0:T(8,128)(2,1)} %all-gather.2.cloned.1.call-done, bf16[1,2048,704]{1,2,0:T(8,128)(2,1)} %param.9), kind=kOutput, calls=%fused_computation.9 | convolution fusion | flops 5905580032 | bytes 17039360 | tf_op jit(solution)/shard_map/dot_general | solution.py:10
  145.5 19.1 %convolution_convert_fusion = bf16[2048,2048]{1,0:T(8,128)(2,1)} fusion(f32[2048,704]{0,1:T(8,128)} %fusion.4, bf16[2048,2048]{1,0:T(8,128)(2,1)} %all-gather.2.cloned.1.call-done, bf16[1,704,2048]{2,1,0:T(8,128)(2,1)S(1)} %copy-done, bf16[1,2048,704]{1,2,0:T(8,128)(2,1)} %param.10), kind=kOutput, calls=%fused_computation.2 | convolution fusion | flops 11824005120 | bytes 28311552 | tf_op jit(solution)/shard_map/dot_general | solution.py:16
  164.6 18.1 %reduce-scatter.2.cloned.1.call-done = bf16[1024,2048]{1,0:T(8,128)(2,1)} async-done(((bf16[2048,2048]{1,0:T(8,128)(2,1)}), bf16[1024,2048]{1,0:T(8,128)(2,1)}) %reduce-scatter.2.cloned.1.call-update) | async-done | bytes 4194320 | tf_op jit(solution)/shard_map/reduce_scatter | solution.py:45
  182.7 6.0 %all-to-all-start.1 = ((bf16[8,128,2048]{2,1,0:T(8,128)(2,1)}), bf16[8,128,2048]{2,1,0:T(8,128)(2,1)}, u32[]{:S(2)}, u32[]{:S(2)}) async-start(bf16[8,128,2048]{2,1,0:T(8,128)(2,1)} %bitcast.41), calls=%async_computation.2 | async-start | bytes 8388608 | tf_op jit(solution)/shard_map/all_to_all | solution.py:49
  188.7 0.1 copy.23
  188.9 0.1 mul.44
  189.0 0.2 copy.22
  189.2 0.1 copy.24
  189.4 93.0 %all-to-all-done.1 = bf16[8,128,2048]{2,1,0:T(8,128)(2,1)} async-done(((bf16[8,128,2048]{2,1,0:T(8,128)(2,1)}), bf16[8,128,2048]{2,1,0:T(8,128)(2,1)}, u32[]{:S(2)}, u32[]{:S(2)}) %all-to-all-start.1) | async-done | bytes 4194336 | tf_op jit(solution)/shard_map/all_to_all | solution.py:49
  282.4 11.6 %gather_fusion = bf16[1024,2048]{1,0:T(8,128)(2,1)} fusion(bf16[1024,2048]{1,0:T(8,128)(2,1)} %bitcast.7, s32[1024]{0:T(1024)S(1)} %broadcast_clamp_fusion), kind=kCustom, calls=%fused_computation | custom fusion | bytes 8392704 | tf_op jit(solution)/shard_map/jit(_take)/gather | solution.py:53
  293.9 7.2 %gather.7 = bf16[256,4,2048]{2,1,0:T(4,128)(2,1)} reshape(bf16[1024,2048]{1,0:T(8,128)(2,1)} %gather_fusion) | data formatting | bytes 8388608 | tf_op jit(solution)/shard_map/jit(_take)/gather | solution.py:53
  301.1 11.0 %multiply_reduce_fusion = bf16[256,2048]{1,0:T(8,128)(2,1)} fusion(f32[256,4]{1,0:T(8,128)S(1)} %copy.24, bf16[256,4,2048]{2,1,0:T(4,128)(2,1)} %gather.7, pred[256,4]{1,0:T(8,128)(4,1)S(1)} %copy.22), kind=kLoop, calls=%fused_computation.1 | loop fusion | flops 7864320 | bytes 5248000 | tf_op jit(solution)/shard_map/reduce_sum | solution.py:54
  (19 shorter events, 0.4 us)
Async XLA Ops:
  6.5 138.9 %copy-start = (bf16[1,704,2048]{2,1,0:T(8,128)(2,1)S(1)}, bf16[1,704,2048]{2,1,0:T(8,128)(2,1)}, u32[]{:S(2)}) copy-start(bf16[1,704,2048]{2,1,0:T(8,128)(2,1)} %param.11) | copy-start | bytes 8650756
  6.5 127.9 %all-gather.2.cloned.1.call-start = ((), (), s32[]{:S(2)}) async-start(), calls=%async_computation.3 | async-start | bytes 12582912 | tf_op jit(solution)/shard_map/all_gather | solution.py:40
  115.4 67.3 %reduce-scatter.2.cloned.1.call-start = ((), (), s32[]{:S(2)}) async-start(), calls=%async_computation.4 | async-start | bytes 12582912 | tf_op jit(solution)/shard_map/reduce_scatter | solution.py:45
  182.7 6.0 %copy-start.1 = (s32[256,4]{0,1:T(4,128)S(1)}, s32[256,4]{0,1:T(4,128)}, u32[]{:S(2)}) copy-start(s32[256,4]{0,1:T(4,128)} %param.7) | copy-start | bytes 12292
  182.7 6.5 %copy-start.2 = (s32[256,4]{0,1:T(4,128)S(1)}, s32[256,4]{0,1:T(4,128)}, u32[]{:S(2)}) copy-start(s32[256,4]{0,1:T(4,128)} %param.8) | copy-start | bytes 12292
  182.7 99.7 %all-to-all-start.1 = ((bf16[8,128,2048]{2,1,0:T(8,128)(2,1)}), bf16[8,128,2048]{2,1,0:T(8,128)(2,1)}, u32[]{:S(2)}, u32[]{:S(2)}) async-start(bf16[8,128,2048]{2,1,0:T(8,128)(2,1)} %bitcast.41), calls=%async_computation.2 | async-start | bytes 8388608 | tf_op jit(solution)/shard_map/all_to_all | solution.py:49
Sparse Core Ops, SparseCore 0:
  115.5 18.8 all-gather.1
  164.7 17.9 reduce-scatter.1
where the time goes:
time: 320 us; the launch traced here: 319 us
  waiting for transfers between devices  130 us (41%)
  blocking collectives  100 us (31%)
  matrix products  32.6 us (10%)
  local copies, waits for them, and re-layouts  21 us (7%)
  other arithmetic  15.3 us (5%)
  between operations  13.5 us (4%)
  starting transfers between devices  6.22 us (2%)
    all_to_all x1, blocking collectives, on_device(): lax.all_to_all(outgoing, 'expert', split_axis=0, concat_axis=0, tiled=True)  100 us
    all_to_all x1, waiting for transfers between devices, on_device(): lax.all_to_all(outputs, 'expert', split_axis=0, concat_axis=0, tiled=True)  93 us
    dot_general x1, matrix products, rounded_term(): jnp.dot(hidden, down_proj, preferred_element_type=jnp.float32)  19.1 us
    all_gather x1, waiting for transfers between devices, on_device(): lax.all_gather(arrived.reshape(experts * capacity, features), 'tensor', a...  18.8 us
    gather x2, local copies, waits for them, and re-layouts, on_device(): jnp.take(flat_back, slot_index.reshape(-1), axis=0)  18.8 us
    reduce_scatter x1, waiting for transfers between devices, on_device(): lax.psum_scatter(term.astype(jnp.float32).astype(jnp.bfloat16), 'tensor',...  18.1 us
    dot_general x1, matrix products, swiglu(): gate_act = jnp.dot(row_block, gate_proj, preferred_element_type=jnp.float32)  11 us
    reduce_sum x1, other arithmetic, on_device(): mixed = jnp.sum(picked.astype(jnp.float32) * weights[:, :, None], axis=1)  11 us
  transfers between devices with their start and end apart: 3, of which 3 were waited for; matrix products, arithmetic and copies ran while one was open for 0% of the time, Pallas kernels for 0%

commit v1 on v0

--- a/solution.py
+++ b/solution.py
@@ -1,9 +1,402 @@
 import jax
 import jax.numpy as jnp
 from jax import lax
+from jax.experimental import pallas as pl
+from jax.experimental.pallas import tpu as pltpu
 from jax.sharding import PartitionSpec as P
 
 TOPK = 4
+LINE = 4
+CHUNKS = 4
+ABSENT = -4096.0
+MESH = pl.DeviceIdType.MESH
+
+
+def moe_kernel(
+    tokens_ref, meta_ref, wg_in, wu_in, wd_in, out_ref,
+    tok, meta, xbuf, ysend, obuf, retsend, csend, cmb, cmbx, wg, wu, wd, hid,
+    own_send, fwd_send, tok_recv, loc_sem, meta_send, meta_recv, w_loc, w_send, w_recv,
+    y_send, y_recv, r_send, r_recv, c_send, c_recv, cx_recv,
+):
+    rows, features = tokens_ref.shape
+    half = rows // 2
+    width = features // CHUNKS
+    experts = meta_ref.shape[0] // 2
+    e = lax.axis_index("expert")
+    t = lax.axis_index("tensor")
+    z = e // 2
+    y = e % 2
+    e_other = z * 2 + (1 - y)
+    h = z // 2
+    m = (1 - h) * z + h * (3 - z)
+    inner = m == 1
+    outer = m == 0
+    z_in = z + 1 - 2 * h
+    z_out = z - (1 - 2 * h) * m
+    src = [(1 - h) * s + h * (3 - s) for s in (m, 1 - m, 2, 3)]
+
+    def zdev(zz):
+        return {"expert": zz * 2 + y}
+
+    ydev = {"expert": e_other}
+    tdev = {"tensor": 1 - t}
+
+    def remote(a, b, ss, rs, dev):
+        return pltpu.make_async_remote_copy(
+            src_ref=a, dst_ref=b, send_sem=ss, recv_sem=rs, device_id=dev, device_id_type=MESH
+        )
+
+    def cols(c):
+        return pl.ds(pl.multiple_of(c * width, width), width)
+
+    barrier = pltpu.get_barrier_semaphore()
+    peers = [zdev((z + d) % LINE) for d in range(1, LINE)] + [ydev, tdev]
+    for dev in peers:
+        pl.semaphore_signal(barrier, inc=1, device_id=dev, device_id_type=MESH)
+    pl.semaphore_wait(barrier, len(peers))
+
+    def own_copy(c, dirn):
+        return remote(
+            tokens_ref.at[:, cols(c)], tok.at[z, c], own_send.at[dirn, c], tok_recv.at[z, c],
+            zdev(z_out if dirn else z_in),
+        )
+
+    def loc_copy(c):
+        return pltpu.make_async_copy(tokens_ref.at[:, cols(c)], tok.at[z, c], loc_sem.at[c])
+
+    def meta_copy(d):
+        return remote(
+            meta_ref, meta.at[z], meta_send.at[d - 1], meta_recv.at[z], zdev((z + d) % LINE)
+        )
+
+    weights = [(wg_in, wg), (wu_in, wu), (wd_in, wd)]
+
+    def w_local(i):
+        return pltpu.make_async_copy(weights[i][0].at[0], weights[i][1].at[t], w_loc.at[i])
+
+    def w_remote(i):
+        return remote(
+            weights[i][0].at[0], weights[i][1].at[t], w_send.at[i], w_recv.at[i], tdev
+        )
+
+    def w_arrival(i):
+        return remote(
+            weights[i][0].at[0], weights[i][1].at[1 - t], w_send.at[i], w_recv.at[i], tdev
+        )
+
+    def each(body):
+        def step(c, carry):
+            body(c)
+            return carry
+
+        lax.fori_loop(0, CHUNKS, step, 0)
+
+    def start_own(c):
+        loc_copy(c).start()
+        own_copy(c, 0).start()
+
+        @pl.when(inner)
+        def _():
+            own_copy(c, 1).start()
+
+    for d in range(1, LINE):
+        meta_copy(d).start()
+    each(start_own)
+    for i in range(3):
+        w_remote(i).start()
+        w_local(i).start()
+    meta[z] = meta_ref[...]
+
+    def arrival(k, c):
+        return remote(
+            tokens_ref.at[:, cols(c)], tok.at[src[k], c], own_send.at[0, c],
+            tok_recv.at[src[k], c], zdev(z_in),
+        )
+
+    def fwd_copy(k, c):
+        return remote(
+            tok.at[src[k], c], tok.at[src[k], c], fwd_send.at[k - 1, c], tok_recv.at[src[k], c],
+            zdev(z_in if k == 1 else z_out),
+        )
+
+    def meta_arrival(k):
+        return remote(
+            meta_ref, meta.at[src[k]], meta_send.at[0], meta_recv.at[src[k]], zdev(z_in)
+        )
+
+    def forward(k, c):
+        @pl.when(inner)
+        def _():
+            arrival(k, c).wait_recv()
+            fwd_copy(k, c).start()
+
+    slot = lax.broadcasted_iota(jnp.int32, (rows, rows), 0)
+    slot_f = slot.astype(jnp.float32)
+
+    def chosen(k):
+        rank_own = meta[src[k], pl.ds(e, 1), :]
+        rank_other = meta[src[k], pl.ds(e_other, 1), :] + float(half)
+        return (slot_f == rank_own) | (slot_f == rank_other)
+
+    def selector(k):
+        return jnp.where(chosen(k), 1.0, 0.0).astype(jnp.bfloat16)
+
+    def mixer(k):
+        weight = jnp.where(
+            slot < half,
+            meta[src[k], pl.ds(experts + e, 1), :],
+            meta[src[k], pl.ds(experts + e_other, 1), :],
+        )
+        spread = jnp.where(chosen(k), weight, 0.0).T
+        high = spread.astype(jnp.bfloat16)
+        low = (spread - high.astype(jnp.float32)).astype(jnp.bfloat16)
+        return high, low
+
+    def y_copy(k, c):
+        return remote(
+            ysend.at[k, c], xbuf.at[k, pl.ds(half, half), cols(c)], y_send.at[k, c],
+            y_recv.at[k, c], ydev,
+        )
+
+    def r_copy(k, c):
+        return remote(
+            retsend.at[k, c], obuf.at[k, c, pl.ds(half, half), :], r_send.at[k, c],
+            r_recv.at[k, c], ydev,
+        )
+
+    def pick(k, c, sel):
+        if k == 0:
+            loc_copy(c).wait()
+        else:
+            @pl.when(outer)
+            def _():
+                arrival(k, c).wait_recv()
+
+        picked = jnp.dot(sel, tok[src[k], c], preferred_element_type=jnp.float32).astype(
+            jnp.bfloat16
+        )
+        xbuf[k, pl.ds(0, half), cols(c)] = picked[:half]
+        ysend[k, c] = picked[half:]
+        y_copy(k, c).start()
+
+    def ffn(k):
+        each(lambda c: y_copy(k, c).wait_recv())
+        for i in range(2):
+            x = xbuf[k]
+            gate = jnp.dot(x, wg[i], preferred_element_type=jnp.float32)
+            up = jnp.dot(x, wu[i], preferred_element_type=jnp.float32)
+            hid[i] = (jax.nn.silu(gate) * up).astype(jnp.bfloat16)
+
+        def down(c):
+            total = jnp.dot(hid[0], wd[0, :, cols(c)], preferred_element_type=jnp.float32)
+            total += jnp.dot(hid[1], wd[1, :, cols(c)], preferred_element_type=jnp.float32)
+            total = total.astype(jnp.bfloat16)
+            obuf[k, c, pl.ds(0, half), :] = total[:half]
+            retsend[k, c] = total[half:]
+            r_copy(k, c).start()
+
+        each(down)
+
+    def mix(k, c, pair):
+        rows_out = obuf[k, c]
+        return jnp.dot(pair[0], rows_out, preferred_element_type=jnp.float32) + jnp.dot(
+            pair[1], rows_out, preferred_element_type=jnp.float32
+        )
+
+    def c_copy(k, c):
+        return remote(
+            csend.at[k - 1, c], cmb.at[src[k], c], c_send.at[k - 1, c], c_recv.at[src[k], c],
+            zdev(z_out if k == 1 else z_in),
+        )
+
+    def cx_copy(c):
+        return remote(csend.at[0, c], cmbx.at[c], c_send.at[0, c], cx_recv.at[c], zdev(z_in))
+
+    def give(k, c, pair):
+        r_copy(k, c).wait_recv()
+        total = mix(k, c, pair)
+
+        @pl.when(outer)
+        def _():
+            csend[k - 1, c] = total.astype(jnp.bfloat16)
+
+        @pl.when(inner)
+        def _():
+            c_copy(k, c).wait_recv()
+            csend[k - 1, c] = (total + cmb[src[k], c].astype(jnp.float32)).astype(jnp.bfloat16)
+
+        c_copy(k, c).start()
+
+    sel0 = selector(0)
+    each(lambda c: pick(0, c, sel0))
+
+    meta_arrival(1).wait_recv()
+    sel1 = selector(1)
+
+    def near(c):
+        forward(1, c)
+        forward(2, c)
+        pick(1, c, sel1)
+
+    each(near)
+    for i in range(3):
+        w_local(i).wait()
+        w_arrival(i).wait_recv()
+    ffn(1)
+
+    @pl.when(outer)
+    def _():
+        pair = mixer(1)
+
+        def send(c):
+            r_copy(1, c).wait_recv()
+            csend[0, c] = mix(1, c, pair).astype(jnp.bfloat16)
+            cx_copy(c).start()
+
+        each(send)
+
+    meta_arrival(2).wait_recv()
+    sel2 = selector(2)
+    each(lambda c: pick(2, c, sel2))
+    each(lambda c: forward(3, c))
+    ffn(0)
+    ffn(2)
+
+    meta_arrival(3).wait_recv()
+    sel3 = selector(3)
+    pair2 = mixer(2)
+
+    def far(c):
+        pick(3, c, sel3)
+        give(2, c, pair2)
+
+    each(far)
+    ffn(3)
+    pair3 = mixer(3)
+    each(lambda c: give(3, c, pair3))
+
+    @pl.when(inner)
+    def _():
+        pair = mixer(1)
+
+        def send(c):
+            r_copy(1, c).wait_recv()
+            total = mix(1, c, pair)
+            c_copy(1, c).wait_recv()
+            csend[0, c] = (total + cmb[src[1], c].astype(jnp.float32)).astype(jnp.bfloat16)
+            c_copy(1, c).start()
+
+        each(send)
+
+    pair0 = mixer(0)
+
+    def finish(c):
+        r_copy(0, c).wait_recv()
+        total = mix(0, c, pair0)
+        remote(
+            csend.at[0, c], cmb.at[z, c], c_send.at[0, c], c_recv.at[z, c], zdev(z_in)
+        ).wait_recv()
+        total = total + cmb[z, c].astype(jnp.float32)
+
+        @pl.when(outer)
+        def _():
+            out_ref[:, cols(c)] = total.astype(jnp.bfloat16)
+
+        @pl.when(inner)
+        def _():
+            cx_copy(c).wait_recv()
+            out_ref[:, cols(c)] = (total + cmbx[c].astype(jnp.float32)).astype(jnp.bfloat16)
+
+    each(finish)
+
+    def drain(c):
+        own_copy(c, 0).wait_send()
+        for k in range(LINE):
+            y_copy(k, c).wait_send()
+            r_copy(k, c).wait_send()
+        for k in (2, 3):
+            c_copy(k, c).wait_send()
+
+        @pl.when(inner)
+        def _():
+            own_copy(c, 1).wait_send()
+            for k in (1, 2, 3):
+                fwd_copy(k, c).wait_send()
+            c_copy(1, c).wait_send()
+
+        @pl.when(outer)
+        def _():
+            cx_copy(c).wait_send()
+
+    each(drain)
+    for d in range(1, LINE):
+        meta_copy(d).wait_send()
+    for i in range(3):
+        w_remote(i).wait_send()
+
+
+def fused(tokens, routes, gates, w_gate, w_up, w_down):
+    rows, features = tokens.shape
+    experts = lax.axis_size("expert")
+    half, width = rows // 2, features // CHUNKS
+    hidden = w_gate.shape[2]
+    weights = gates.astype(jnp.float32)
+    weights = weights / jnp.sum(weights, axis=1, keepdims=True)
+    names = routes[:, :, None] == jnp.arange(experts, dtype=jnp.int32)[None, None, :]
+    weight_of = jnp.sum(jnp.where(names, weights[:, :, None], 0.0), axis=1).T
+    chosen = jnp.any(names, axis=1).T
+    place = jnp.arange(rows, dtype=jnp.int32)
+    earlier = (place[:, None] < place[None, :]).astype(jnp.bfloat16)
+    rank = jnp.dot(chosen.astype(jnp.bfloat16), earlier, preferred_element_type=jnp.float32)
+    meta = jnp.concatenate([jnp.where(chosen, rank, ABSENT), weight_of], axis=0)
+    bf16, dma = jnp.bfloat16, pltpu.SemaphoreType.DMA
+    return pl.pallas_call(
+        moe_kernel,
+        out_shape=jax.ShapeDtypeStruct((rows, features), bf16),
+        in_specs=[
+            pl.BlockSpec(memory_space=pl.ANY),
+            pl.BlockSpec(memory_space=pltpu.VMEM),
+            pl.BlockSpec(memory_space=pl.ANY),
+            pl.BlockSpec(memory_space=pl.ANY),
+            pl.BlockSpec(memory_space=pl.ANY),
+        ],
+        out_specs=pl.BlockSpec(memory_space=pltpu.VMEM),
+        scratch_shapes=[
+            pltpu.VMEM((LINE, CHUNKS, rows, width), bf16),
+            pltpu.VMEM((LINE, 2 * experts, rows), jnp.float32),
+            pltpu.VMEM((LINE, rows, features), bf16),
+            pltpu.VMEM((LINE, CHUNKS, half, width), bf16),
+            pltpu.VMEM((LINE, CHUNKS, rows, width), bf16),
+            pltpu.VMEM((LINE, CHUNKS, half, width), bf16),
+            pltpu.VMEM((LINE - 1, CHUNKS, rows, width), bf16),
+            pltpu.VMEM((LINE, CHUNKS, rows, width), bf16),
+            pltpu.VMEM((CHUNKS, rows, width), bf16),
+            pltpu.VMEM((2, features, hidden), bf16),
+            pltpu.VMEM((2, features, hidden), bf16),
+            pltpu.VMEM((2, hidden, features), bf16),
+            pltpu.VMEM((2, rows, hidden), bf16),
+            dma((2, CHUNKS)),
+            dma((LINE - 1, CHUNKS)),
+            dma((LINE, CHUNKS)),
+            dma((CHUNKS,)),
+            dma((LINE - 1,)),
+            dma((LINE,)),
+            dma((3,)),
+            dma((3,)),
+            dma((3,)),
+            dma((LINE, CHUNKS)),
+            dma((LINE, CHUNKS)),
+            dma((LINE, CHUNKS)),
+            dma((LINE, CHUNKS)),
+            dma((LINE - 1, CHUNKS)),
+            dma((LINE, CHUNKS)),
+            dma((CHUNKS,)),
+        ],
+        compiler_params=pltpu.CompilerParams(
+            collective_id=0, has_side_effects=True, vmem_limit_bytes=56 * 1024 * 1024
+        ),
+        name="moe",
+    )(tokens, meta, w_gate, w_up, w_down)
 
 
 def swiglu(row_block, gate_proj, up_proj):
@@ -65,6 +458,7 @@
         P("expert", "tensor", None),
     )
     out_specs = P(("groups", "expert", "tensor"), None)
+    paired = mesh.shape["expert"] == 2 * LINE and mesh.shape["tensor"] == 2
     return jax.shard_map(
-        on_device, mesh=mesh, in_specs=in_specs, out_specs=out_specs, check_vma=False
-    )
+        fused if paired else on_device, mesh=mesh, in_specs=in_specs, out_specs=out_specs, check_vma=False
+    )

time: 320 us -> 161 us (0.50)
  Pallas kernels: 0 us -> 147 us
  waiting for transfers between devices: 130 us -> 0 us
  blocking collectives: 100 us -> 0 us
  matrix products: 32.6 us -> 0.15 us
  between operations: 13.5 us -> 0.01 us
  other arithmetic: 15.3 us -> 3.41 us
  local copies, waits for them, and re-layouts: 21 us -> 9.88 us
  starting transfers between devices: 6.22 us -> 0 us
    pallas_call x0 -> x1, Pallas kernels: none -> 147 us  [fused(): pl.pallas_call(moe_kernel, out_shape=jax.ShapeDtypeStruct((rows, features...]
    all_to_all x1 -> x0, blocking collectives: 100 us -> none  [on_device(): lax.all_to_all(outgoing, 'expert', split_axis=0, concat_axis=0, tiled=True)]
    all_to_all x1 -> x0, waiting for transfers between devices: 93 us -> none  [on_device(): lax.all_to_all(outputs, 'expert', split_axis=0, concat_axis=0, tiled=True)]
    dot_general x3 -> x1, matrix products: 32.6 us -> 0.15 us  [fused(): jnp.dot(chosen.astype(jnp.bfloat16), earlier, preferred_element_type=jnp....]
    all_gather x1 -> x0, waiting for transfers between devices: 18.8 us -> none  [on_device(): lax.all_gather(arrived.reshape(experts * capacity, features), 'tensor', a...]
    gather x2 -> x0, local copies, waits for them, and re-layouts: 18.8 us -> none  [on_device(): jnp.take(flat_back, slot_index.reshape(-1), axis=0)]
    reduce_scatter x1 -> x0, waiting for transfers between devices: 18.1 us -> none  [on_device(): lax.psum_scatter(term.astype(jnp.float32).astype(jnp.bfloat16), 'tensor',...]
    reduce_sum x3 -> x2, other arithmetic: 11.1 us -> 1.4 us  [the longest x1 0.7 us: fused(): weights = weights / jnp.sum(weights, axis=1, keepdims=True)]
  transfers between devices with their start and end apart: 3 -> 0, of which waited for: 3 -> 0; matrix products, arithmetic and copies ran while one was open for 0% -> 0% of each run, Pallas kernels for 0% -> 0%
where the time goes in v1:
time: 161 us; the launch traced here: 160 us
  Pallas kernels  147 us (91%)
  local copies, waits for them, and re-layouts  9.88 us (6%)
  other arithmetic  3.41 us (2%)
    pallas_call x1, Pallas kernels, fused(): pl.pallas_call(moe_kernel, out_shape=jax.ShapeDtypeStruct((rows, features...  147 us
    unnamed x5, local copies, waits for them, and re-layouts  9.88 us

profile of v1, /device:TPU:0, one launch (start us, length us, event | category | flops | bytes accessed | tf_op | source)
XLA Modules:
  0.0 160.2 jit_solution(1871356009149700475)
XLA Ops:
  0.0 0.7 convert_reduce_fusion
  0.7 0.7 fusion
  1.4 0.7 convert_divide_fusion
  2.1 0.7 select_reduce_fusion
  2.8 0.1 convolution_select_fusion
  2.9 0.6 pad_maximum_fusion.meta_ref
  3.6 0.0 copy-start
  3.6 4.7 %copy.11.wg_in = bf16[1,2048,704]{2,1,0:T(8,128)(2,1)} copy(bf16[1,2048,704]{1,2,0:T(8,128)(2,1)} %param.9) | data formatting | bytes 5767168 | tf_op args[3]
  8.3 0.0 copy-done
  8.3 2.8 %copy.12.wu_in = bf16[1,2048,704]{2,1,0:T(8,128)(2,1)} copy(bf16[1,2048,704]{1,2,0:T(8,128)(2,1)S(1)} %copy-done) | data formatting | bytes 5767168 | tf_op args[4]
  11.1 146.8 %moe.1 = bf16[256,2048]{1,0:T(8,128)(2,1)} custom-call(bf16[256,2048]{1,0:T(8,128)(2,1)} %tokens_ref.1, f32[16,256]{1,0:T(8,128)} %pad_maximum_fusion.meta_ref, bf16[1,2048,704]{2,1,0:T(8,128)(2,1)} %copy.11.wg_in, bf16[1,2048,704]{2,1,0:T(8,128)(2,1)} %copy.12.wu_in, bf16[1,704,2048]{2,1,0:T(8,128)(2,1)} %wd_in.1), custom_call_target="tpu_custom_call" | custom-call | tf_op jit(solution)/shard_map/moe/pallas_call | solution.py:353
  157.9 2.3 %copy.14 = bf16[256,2048]{1,0:T(8,128)(2,1)} copy(bf16[256,2048]{1,0:T(8,128)(2,1)} %moe.1) | data formatting | bytes 2097152
Async XLA Ops:
  3.6 4.7 %copy-start = (bf16[1,2048,704]{1,2,0:T(8,128)(2,1)S(1)}, bf16[1,2048,704]{1,2,0:T(8,128)(2,1)}, u32[]{:S(2)}) copy-start(bf16[1,2048,704]{1,2,0:T(8,128)(2,1)} %param.10) | copy-start | bytes 8650756

commit v2 on v1

--- a/solution.py
+++ b/solution.py
@@ -9,11 +9,12 @@
 LINE = 4
 CHUNKS = 4
 ABSENT = -4096.0
+LAST = (((1,), (1,)), ((), ()))
 MESH = pl.DeviceIdType.MESH
 
 
 def moe_kernel(
-    tokens_ref, meta_ref, wg_in, wu_in, wd_in, out_ref,
+    tokens_ref, routes_ref, gates_ref, wg_in, wu_in, wd_in, out_ref,
     tok, meta, xbuf, ysend, obuf, retsend, csend, cmb, cmbx, wg, wu, wd, hid,
     own_send, fwd_send, tok_recv, loc_sem, meta_send, meta_recv, w_loc, w_send, w_recv,
     y_send, y_recv, r_send, r_recv, c_send, c_recv, cx_recv,
@@ -21,7 +22,7 @@
     rows, features = tokens_ref.shape
     half = rows // 2
     width = features // CHUNKS
-    experts = meta_ref.shape[0] // 2
+    experts = meta.shape[1] // 2
     e = lax.axis_index("expert")
     t = lax.axis_index("tensor")
     z = e // 2
@@ -66,22 +67,22 @@
 
     def meta_copy(d):
         return remote(
-            meta_ref, meta.at[z], meta_send.at[d - 1], meta_recv.at[z], zdev((z + d) % LINE)
+            meta.at[z], meta.at[z], meta_send.at[d - 1], meta_recv.at[z], zdev((z + d) % LINE)
         )
 
     weights = [(wg_in, wg), (wu_in, wu), (wd_in, wd)]
 
     def w_local(i):
-        return pltpu.make_async_copy(weights[i][0].at[0], weights[i][1].at[t], w_loc.at[i])
+        return pltpu.make_async_copy(weights[i][0], weights[i][1].at[t], w_loc.at[i])
 
     def w_remote(i):
         return remote(
-            weights[i][0].at[0], weights[i][1].at[t], w_send.at[i], w_recv.at[i], tdev
+            weights[i][0], weights[i][1].at[t], w_send.at[i], w_recv.at[i], tdev
         )
 
     def w_arrival(i):
         return remote(
-            weights[i][0].at[0], weights[i][1].at[1 - t], w_send.at[i], w_recv.at[i], tdev
+            weights[i][0], weights[i][1].at[1 - t], w_send.at[i], w_recv.at[i], tdev
         )
 
     def each(body):
@@ -99,13 +100,28 @@
         def _():
             own_copy(c, 1).start()
 
-    for d in range(1, LINE):
-        meta_copy(d).start()
     each(start_own)
     for i in range(3):
         w_remote(i).start()
         w_local(i).start()
-    meta[z] = meta_ref[...]
+
+    gate = gates_ref[...].astype(jnp.float32)
+    gate = gate / jnp.sum(gate, axis=0, keepdims=True)
+    expert_of = lax.broadcasted_iota(jnp.int32, (experts, rows), 0)
+    weight_of = jnp.zeros((experts, rows), jnp.float32)
+    named = jnp.zeros((experts, rows), jnp.float32)
+    for k in range(TOPK):
+        match = expert_of == routes_ref[k : k + 1, :]
+        weight_of = jnp.where(match, gate[k : k + 1, :], weight_of)
+        named = jnp.where(match, 1.0, named)
+    before = lax.broadcasted_iota(jnp.int32, (rows, rows), 0)
+    after = lax.broadcasted_iota(jnp.int32, (rows, rows), 1)
+    earlier = jnp.where(before < after, 1.0, 0.0).astype(jnp.bfloat16)
+    rank = jnp.dot(named.astype(jnp.bfloat16), earlier, preferred_element_type=jnp.float32)
+    meta[z, pl.ds(0, experts), :] = jnp.where(named > 0.5, rank, ABSENT)
+    meta[z, pl.ds(experts, experts), :] = weight_of
+    for d in range(1, LINE):
+        meta_copy(d).start()
 
     def arrival(k, c):
         return remote(
@@ -121,7 +137,7 @@
 
     def meta_arrival(k):
         return remote(
-            meta_ref, meta.at[src[k]], meta_send.at[0], meta_recv.at[src[k]], zdev(z_in)
+            meta.at[z], meta.at[src[k]], meta_send.at[0], meta_recv.at[src[k]], zdev(z_in)
         )
 
     def forward(k, c):
@@ -183,8 +199,8 @@
         each(lambda c: y_copy(k, c).wait_recv())
         for i in range(2):
             x = xbuf[k]
-            gate = jnp.dot(x, wg[i], preferred_element_type=jnp.float32)
-            up = jnp.dot(x, wu[i], preferred_element_type=jnp.float32)
+            gate = lax.dot_general(x, wg[i], LAST, preferred_element_type=jnp.float32)
+            up = lax.dot_general(x, wu[i], LAST, preferred_element_type=jnp.float32)
             hid[i] = (jax.nn.silu(gate) * up).astype(jnp.bfloat16)
 
         def down(c):
@@ -244,22 +260,21 @@
         w_arrival(i).wait_recv()
     ffn(1)
 
-    @pl.when(outer)
-    def _():
-        pair = mixer(1)
-
-        def send(c):
-            r_copy(1, c).wait_recv()
-            csend[0, c] = mix(1, c, pair).astype(jnp.bfloat16)
-            cx_copy(c).start()
-
-        each(send)
-
     meta_arrival(2).wait_recv()
     sel2 = selector(2)
-    each(lambda c: pick(2, c, sel2))
+    pair1 = mixer(1)
+
+    def second(c):
+        @pl.when(outer)
+        def _():
+            r_copy(1, c).wait_recv()
+            csend[0, c] = mix(1, c, pair1).astype(jnp.bfloat16)
+            cx_copy(c).start()
+
+        pick(2, c, sel2)
+
+    each(second)
     each(lambda c: forward(3, c))
-    ffn(0)
     ffn(2)
 
     meta_arrival(3).wait_recv()
@@ -273,20 +288,32 @@
     each(far)
     ffn(3)
     pair3 = mixer(3)
-    each(lambda c: give(3, c, pair3))
+
+    @pl.when(outer)
+    def _():
+        each(lambda c: give(3, c, pair3))
+        ffn(0)
 
     @pl.when(inner)
     def _():
-        pair = mixer(1)
-
-        def send(c):
+        ffn(0)
+
+        def last_hop(c):
             r_copy(1, c).wait_recv()
-            total = mix(1, c, pair)
+            total = mix(1, c, pair1)
             c_copy(1, c).wait_recv()
             csend[0, c] = (total + cmb[src[1], c].astype(jnp.float32)).astype(jnp.bfloat16)
             c_copy(1, c).start()
 
-        each(send)
+        give(3, 0, pair3)
+
+        def step(c, carry):
+            give(3, c, pair3)
+            last_hop(c - 1)
+            return carry
+
+        lax.fori_loop(1, CHUNKS, step, 0)
+        last_hop(CHUNKS - 1)
 
     pair0 = mixer(0)
 
@@ -340,21 +367,13 @@
     experts = lax.axis_size("expert")
     half, width = rows // 2, features // CHUNKS
     hidden = w_gate.shape[2]
-    weights = gates.astype(jnp.float32)
-    weights = weights / jnp.sum(weights, axis=1, keepdims=True)
-    names = routes[:, :, None] == jnp.arange(experts, dtype=jnp.int32)[None, None, :]
-    weight_of = jnp.sum(jnp.where(names, weights[:, :, None], 0.0), axis=1).T
-    chosen = jnp.any(names, axis=1).T
-    place = jnp.arange(rows, dtype=jnp.int32)
-    earlier = (place[:, None] < place[None, :]).astype(jnp.bfloat16)
-    rank = jnp.dot(chosen.astype(jnp.bfloat16), earlier, preferred_element_type=jnp.float32)
-    meta = jnp.concatenate([jnp.where(chosen, rank, ABSENT), weight_of], axis=0)
     bf16, dma = jnp.bfloat16, pltpu.SemaphoreType.DMA
     return pl.pallas_call(
         moe_kernel,
         out_shape=jax.ShapeDtypeStruct((rows, features), bf16),
         in_specs=[
             pl.BlockSpec(memory_space=pl.ANY),
+            pl.BlockSpec(memory_space=pltpu.VMEM),
             pl.BlockSpec(memory_space=pltpu.VMEM),
             pl.BlockSpec(memory_space=pl.ANY),
             pl.BlockSpec(memory_space=pl.ANY),
@@ -371,8 +390,8 @@
             pltpu.VMEM((LINE - 1, CHUNKS, rows, width), bf16),
             pltpu.VMEM((LINE, CHUNKS, rows, width), bf16),
             pltpu.VMEM((CHUNKS, rows, width), bf16),
-            pltpu.VMEM((2, features, hidden), bf16),
-            pltpu.VMEM((2, features, hidden), bf16),
+            pltpu.VMEM((2, hidden, features), bf16),
+            pltpu.VMEM((2, hidden, features), bf16),
             pltpu.VMEM((2, hidden, features), bf16),
             pltpu.VMEM((2, rows, hidden), bf16),
             dma((2, CHUNKS)),
@@ -396,7 +415,7 @@
             collective_id=0, has_side_effects=True, vmem_limit_bytes=56 * 1024 * 1024
         ),
         name="moe",
-    )(tokens, meta, w_gate, w_up, w_down)
+    )(tokens, routes.T, gates.T, w_gate[0].T, w_up[0].T, w_down[0])
 
 
 def swiglu(row_block, gate_proj, up_proj):

time: 161 us -> 143 us (0.89)
  local copies, waits for them, and re-layouts: 9.88 us -> 2.3 us
  Pallas kernels: 147 us -> 141 us
  other arithmetic: 3.41 us -> 0 us
    unnamed x5 -> x1, local copies, waits for them, and re-layouts: 9.88 us -> 2.3 us
    pallas_call x1, Pallas kernels: 147 us -> 141 us  [fused(): pl.pallas_call(moe_kernel, out_shape=jax.ShapeDtypeStruct((rows, features...]
where the time goes in v2:
time: 143 us
  Pallas kernels  141 us (99%)
  local copies, waits for them, and re-layouts  2.3 us (2%)
    pallas_call x1, Pallas kernels, fused(): pl.pallas_call(moe_kernel, out_shape=jax.ShapeDtypeStruct((rows, features...  141 us

profile of v2, /device:TPU:0, one launch (start us, length us, event | category | flops | bytes accessed | tf_op | source)
XLA Modules:
  0.0 143.0 jit_solution(8318413441935683603)
XLA Ops:
  0.0 140.6 %moe.1 = bf16[256,2048]{1,0:T(8,128)(2,1)} custom-call(bf16[256,2048]{1,0:T(8,128)(2,1)} %tokens_ref.1, s32[4,256]{1,0:T(4,128)} %bitcast.12, s32[4,256]{1,0:T(4,128)} %bitcast.13, bf16[704,2048]{1,0:T(8,128)(2,1)} %bitcast.9, bf16[704,2048]{1,0:T(8,128)(2,1)} %bitcast.10, bf16[704,2048]{1,0:T(8,128)(2,1)} %bitcast.11), custom_call_target="tpu_custom_call" | custom-call | tf_op jit(solution)/shard_map/moe/pallas_call | solution.py:371
  140.7 2.3 %copy.8 = bf16[256,2048]{1,0:T(8,128)(2,1)} copy(bf16[256,2048]{1,0:T(8,128)(2,1)} %moe.1) | data formatting | bytes 2097152

commit v3 on v2

--- a/solution.py
+++ b/solution.py
@@ -199,9 +199,9 @@
         each(lambda c: y_copy(k, c).wait_recv())
         for i in range(2):
             x = xbuf[k]
-            gate = lax.dot_general(x, wg[i], LAST, preferred_element_type=jnp.float32)
-            up = lax.dot_general(x, wu[i], LAST, preferred_element_type=jnp.float32)
-            hid[i] = (jax.nn.silu(gate) * up).astype(jnp.bfloat16)
+            gate = lax.dot_general(wg[i], x, LAST, preferred_element_type=jnp.float32)
+            up = lax.dot_general(wu[i], x, LAST, preferred_element_type=jnp.float32)
+            hid[i] = (jax.nn.silu(gate) * up).T.astype(jnp.bfloat16)
 
         def down(c):
             total = jnp.dot(hid[0], wd[0, :, cols(c)], preferred_element_type=jnp.float32)

time: 143 us -> 142 us (level)
  no operation moved by 1% of the time
where the time goes in v3:
time: 142 us
  Pallas kernels  140 us (99%)
  local copies, waits for them, and re-layouts  2.3 us (2%)
    pallas_call x1, Pallas kernels, fused(): pl.pallas_call(moe_kernel, out_shape=jax.ShapeDtypeStruct((rows, features...  140 us

profile of v3, /device:TPU:0, one launch (start us, length us, event | category | flops | bytes accessed | tf_op | source)
XLA Modules:
  0.0 142.0 jit_solution(6378491842942496491)
XLA Ops:
  0.0 139.7 %moe.1 = bf16[256,2048]{1,0:T(8,128)(2,1)} custom-call(bf16[256,2048]{1,0:T(8,128)(2,1)} %tokens_ref.1, s32[4,256]{1,0:T(4,128)} %bitcast.12, s32[4,256]{1,0:T(4,128)} %bitcast.13, bf16[704,2048]{1,0:T(8,128)(2,1)} %bitcast.9, bf16[704,2048]{1,0:T(8,128)(2,1)} %bitcast.10, bf16[704,2048]{1,0:T(8,128)(2,1)} %bitcast.11), custom_call_target="tpu_custom_call" | custom-call | tf_op jit(solution)/shard_map/moe/pallas_call | solution.py:371
  139.7 2.3 %copy.8 = bf16[256,2048]{1,0:T(8,128)(2,1)} copy(bf16[256,2048]{1,0:T(8,128)(2,1)} %moe.1) | data formatting | bytes 2097152
